TPU v7x, 32 devices: a whole 2x2x4 slice. The times are simulated.
32 devices in a mesh: dp: 4 (over x, core), blk: 4 (over z), resp: 2 (over y).
Axes of the slice: x: 2, y: 2, z: 4, core: 2. Of those that a mesh axis runs over, the one named last changes fastest.
Arguments:
- saved: bfloat16 [4, 512, 3, 1280], P('dp', 'blk', None, 'resp'), may hold values from -24 to 24
- prefix_cot: bfloat16 [4, 2, 512, 1280], P('dp', 'resp', 'blk'), may hold values from -24 to 24
- w_out: bfloat16 [1280, 1280], P('resp'), may hold values from -0.15625 to 0.15625
- lengths: int32 [4, 4], P('dp', 'resp'), may hold values from 1 to 512, 1024 in all within a row
- adv_mask: int32 [4, 4, 512], P('dp', 'resp'), may hold values from -3 to 3, as said below
- patch_map: int32 [4, 4, 128], P('dp', 'blk'), may hold values from 0 to 127, each once within a row
Outputs:
- grad_qkv: bfloat16 [4, 512, 3, 1280], P('dp', 'blk', None, 'resp')
Inputs may be any that keep to these rules, and one draw needn't show every extreme that they name: `adv_mask`: within one response every nonzero entry has the same value. The 4 lengths of one image sum to 1024; the longest is 512. `patch_map`: each row of 128 entries holds every number of 0 to 127 once.
All inputs are finite; a program needn't handle non-finite values. No bound on the sum of `lengths` on one device may be relied on, other than what follows from the above.
Results may differ from a plain program's by a relative error of at most 0.03.
Values may be sent and summed in bfloat16 or wider, within the bound.
A program may use at most 64 MiB of HBM per device.

v0:
```python
import math

import jax
import jax.numpy as jnp
from jax import lax
from jax.sharding import PartitionSpec as P

HD = 80
MAXLEN = 512


def score_pair(query, grad, log_total, delta, keys, values, scale):
    score = jnp.einsum("qhd,khd->hqk", query, keys, preferred_element_type=jnp.float32) * scale
    prob = jnp.exp(score - log_total[:, :, None])
    dprob = jnp.einsum("qhd,khd->hqk", grad, values, preferred_element_type=jnp.float32)
    dscore = (prob * (dprob - delta[:, :, None])).astype(jnp.bfloat16)
    return (prob.astype(jnp.bfloat16), dscore)


def shards(saved, prefix_cot, w_out, lengths, adv_mask, patch_map):
    rows = saved.shape[1]
    width = saved.shape[3]
    heads_here = width // HD
    scale = 1.0 / math.sqrt(HD)
    live = lax.broadcasted_iota(jnp.int32, adv_mask.shape, 2) < lengths[:, :, None]
    resp_weight = jnp.sum(jnp.where(live, adv_mask, 0).astype(jnp.float32), axis=2) / MAXLEN
    group_weight = jnp.sum(resp_weight)
    share = lax.psum_scatter(
        (group_weight * prefix_cot[0, 0].astype(jnp.float32)).astype(jnp.bfloat16),
        "resp",
        scatter_dimension=0,
        tiled=True,
    )
    total = lax.all_gather(share, "resp", axis=0, tiled=True)
    cot_rows = jnp.take(total, patch_map[0, 0], axis=0)
    grad_out = lax.dot_general(
        cot_rows, w_out, (((1,), (1,)), ((), ())), preferred_element_type=jnp.float32
    ).astype(jnp.bfloat16)
    query = saved[0, :, 0, :].reshape(rows, heads_here, HD)
    keys = saved[0, :, 1, :].reshape(rows, heads_here, HD)
    values = saved[0, :, 2, :].reshape(rows, heads_here, HD)
    grad = grad_out.reshape(rows, heads_here, HD)
    key_value = saved[0, :, 1:, :].reshape(rows, 2 * width)
    piece = lax.all_gather(key_value, "blk", axis=0, tiled=True)
    top = jnp.full((heads_here, rows), -1e30, jnp.float32)
    count = piece.shape[0]
    key_part = piece[:, :width].reshape(count, heads_here, HD)
    value_part = piece[:, width:].reshape(count, heads_here, HD)
    score = jnp.einsum("qhd,khd->hqk", query, key_part, preferred_element_type=jnp.float32) * scale
    new_top = jnp.maximum(top, jnp.max(score, axis=2))
    expo = jnp.exp(score - new_top[:, :, None])
    row_total = jnp.sum(expo, axis=2)
    accum = jnp.einsum(
        "hqk,khd->hqd", expo.astype(jnp.bfloat16), value_part, preferred_element_type=jnp.float32
    )
    top, row_total, accum = (new_top, row_total, accum)
    output = (accum / row_total[:, :, None]).astype(jnp.bfloat16)
    log_total = top + jnp.log(row_total)
    delta = jnp.einsum("qhd,hqd->hq", grad, output, preferred_element_type=jnp.float32)
    packed = jnp.concatenate([saved[0], grad_out[:, None, :]], axis=1).reshape(rows, 4 * width)
    stats = jnp.concatenate([log_total, delta], axis=0).T
    block = lax.all_gather(packed.astype(jnp.float32), "blk", axis=0, tiled=True).astype(
        jnp.bfloat16
    )
    stat_block = lax.all_gather(stats, "blk", axis=0, tiled=True)
    count = block.shape[0]
    far_q = block[:, :width].reshape(count, heads_here, HD)
    far_k = block[:, width : 2 * width].reshape(count, heads_here, HD)
    far_v = block[:, 2 * width : 3 * width].reshape(count, heads_here, HD)
    far_g = block[:, 3 * width :].reshape(count, heads_here, HD)
    far_log = stat_block[:, :heads_here].T
    far_delta = stat_block[:, heads_here:].T
    near_prob, near_ds = score_pair(query, grad, log_total, delta, far_k, far_v, scale)
    grad_q = jnp.einsum("hqk,khd->hqd", near_ds, far_k, preferred_element_type=jnp.float32) * scale
    far_prob, far_ds = score_pair(far_q, far_g, far_log, far_delta, keys, values, scale)
    grad_k = jnp.einsum("hqk,qhd->khd", far_ds, far_q, preferred_element_type=jnp.float32) * scale
    grad_v = jnp.einsum("hqk,qhd->khd", far_prob, far_g, preferred_element_type=jnp.float32)
    grad_q, grad_k, grad_v = (grad_q, grad_k, grad_v)
    grad_k = grad_k.reshape(rows, width)
    grad_v = grad_v.reshape(rows, width)
    grad_q = grad_q.transpose(1, 0, 2).reshape(rows, width)
    result = jnp.stack([grad_q, grad_k, grad_v], axis=1).astype(jnp.bfloat16)
    return result[None]


def solution(mesh):
    in_specs = (
        P("dp", "blk", None, "resp"),
        P("dp", "resp", "blk", None),
        P("resp", None),
        P("dp", "resp"),
        P("dp", "resp", None),
        P("dp", "blk", None),
    )
    out_specs = P("dp", "blk", None, "resp")
    return jax.shard_map(shards, mesh=mesh, in_specs=in_specs, out_specs=out_specs, check_vma=False)
```

profile of v0, /device:TPU:0, one launch (start us, length us, event | category | flops | bytes accessed | tf_op | source)
XLA Modules:
  0.0 129.5 jit_solution(3914325285969982640)
XLA Ops:
  7.4 0.0 copy-start
  7.4 0.0 reduce-scatter.2.cloned.1.call-start
  7.4 1.0 fusion.31
  8.4 0.7 multiply_reduce_fusion.1
  9.0 2.4 %fusion.26 = bf16[128,1280]{1,0:T(8,128)(2,1)} fusion(bf16[1,1,128,1280]{3,2,1,0:T(8,128)(2,1)} %param.7, f32[]{:T(128)} %multiply_reduce_fusion.1), kind=kLoop, calls=%fused_computation.37 | loop fusion | flops 491520 | bytes 655364 | tf_op jit(solution)/shard_map/convert_element_type | solution.py:29
  11.4 0.0 reduce-scatter.2.cloned.1.call-update
  11.5 0.0 all-gather.5.cloned.1.call-start
  11.5 1.3 %copy.13 = bf16[1,128,3,640]{1,3,2,0:T(8,128)(2,1)S(1)} copy(bf16[1,128,3,640]{3,1,2,0:T(8,128)(2,1)} %param.6) | data formatting | bytes 983040 | tf_op args[0]
  12.8 0.8 slice.51
  13.6 0.0 all-gather.5.cloned.1.call-update
  13.6 0.0 all-gather.3.cloned.1.call-start
  13.6 0.0 copy-done.5
  13.7 13.0 %reduce-scatter.2.cloned.1.call-done = bf16[64,1280]{1,0:T(8,128)(2,1)} async-done(((bf16[128,1280]{1,0:T(8,128)(2,1)}), bf16[64,1280]{1,0:T(8,128)(2,1)}) %reduce-scatter.2.cloned.1.call-update) | async-done | bytes 163856 | tf_op jit(solution)/shard_map/reduce_scatter | solution.py:28
  26.7 6.8 %all_gather.12 = bf16[128,1280]{1,0:T(8,128)(2,1)S(1)} all-gather(bf16[64,1280]{1,0:T(8,128)(2,1)} %reduce-scatter.2.cloned.1.call-done), channel_id=1, replica_groups=mesh['dp'=4,'blk'=4,'resp'=2] {'resp'}, dimensions={0}, use_global_device_ids=true | all-gather | bytes 491520 | tf_op jit(solution)/shard_map/all_gather | solution.py:34
  33.5 0.9 gather_fusion
  34.4 0.0 copy-done
  34.4 0.0 copy-start.3
  34.5 0.6 convolution_convert_fusion.1
  35.1 0.2 copy.14
  35.3 0.9 pad_maximum_fusion
  36.2 0.0 all-gather.3.cloned.1.call-update
  36.2 0.7 slice.58
  36.9 0.0 copy-done.3
  36.9 0.2 copy.15
  37.1 0.2 copy.19
  37.2 0.2 copy.17
  37.4 0.1 copy.28
  37.6 12.1 %all-gather.5.cloned.1.call-done = bf16[512,1280]{0,1:T(8,128)(2,1)} async-done(((bf16[128,1280]{0,1:T(8,128)(2,1)}), bf16[512,1280]{0,1:T(8,128)(2,1)}) %all-gather.5.cloned.1.call-update) | async-done | bytes 1310736 | tf_op jit(solution)/shard_map/all_gather | solution.py:44
  49.7 1.4 %fusion.39 = (bf16[512,640]{0,1:T(8,128)(2,1)S(1)}, bf16[512,640]{0,1:T(8,128)(2,1)S(1)}) fusion(bf16[512,1280]{0,1:T(8,128)(2,1)} %all-gather.5.cloned.1.call-done), kind=kLoop, calls=%fused_computation.61 | loop fusion | bytes 2621440 | tf_op jit(solution)/shard_map/slice | solution.py:47
  51.1 0.6 multiply_reduce_fusion
  51.6 0.6 fusion.2
  52.2 0.8 fusion.11
  53.0 13.2 %all_gather.15 = f32[512,16]{0,1:T(8,128)S(1)} all-gather(f32[128,16]{0,1:T(8,128)S(1)} %maximum_bitcast_fusion), channel_id=1, replica_groups=mesh['dp'=4,'blk'=4,'resp'=2] {'blk'}, dimensions={0}, use_global_device_ids=true | all-gather | bytes 40960 | tf_op jit(solution)/shard_map/all_gather | solution.py:65
  66.2 38.3 %all-gather.3.cloned.1.call-done = bf16[512,2560]{0,1:T(8,128)(2,1)} async-done(((bf16[128,2560]{0,1:T(8,128)(2,1)}), bf16[512,2560]{0,1:T(8,128)(2,1)}) %all-gather.3.cloned.1.call-update) | async-done | bytes 2621456 | tf_op jit(solution)/shard_map/all_gather | solution.py:62
  104.5 2.8 %fusion.38 = (bf16[512,640]{0,1:T(8,128)(2,1)}, bf16[512,640]{0,1:T(8,128)(2,1)S(1)}, bf16[512,640]{0,1:T(8,128)(2,1)S(1)}, bf16[512,640]{0,1:T(8,128)(2,1)S(1)}) fusion(bf16[512,2560]{0,1:T(8,128)(2,1)} %all-gather.3.cloned.1.call-done), kind=kLoop, calls=%fused_computation.60 | loop fusion | bytes 5242880 | tf_op jit(solution)/shard_map/slice | solution.py:69
  107.3 0.8 copy-done.2
  108.2 1.8 %fusion.41 = f32[8,512,128]{2,1,0:T(8,128)} fusion(bf16[512,8,80]{0,2,1:T(8,128)(2,1)S(1)} %bitcast.75, bf16[128,8,80]{0,2,1:T(8,128)(2,1)S(1)} %bitcast.79), kind=kOutput, calls=%fused_computation.63 | convolution fusion | flops 83886080 | bytes 2916352 | tf_op jit(solution)/shard_map/qhd,khd->hqk/dot_general | solution.py:13
  110.0 3.0 %fusion.13 = bf16[8,128,80]{1,2,0:T(8,128)(2,1)S(1)} fusion(bf16[512,8,80]{0,2,1:T(8,128)(2,1)} %bitcast.76, f32[8,512,128]{2,1,0:T(8,128)} %fusion.41, bf16[128,8,80]{0,2,1:T(8,128)(2,1)S(1)} %bitcast.87, bf16[512,8,80]{0,2,1:T(8,128)(2,1)} %bitcast.85, f32[8,128]{1,0:T(8,128)S(1)} %fusion.11, f32[8,128]{1,0:T(8,128)S(1)} %log_add_fusion), kind=kOutput, calls=%fused_computation.20 | convolution fusion | flops 170557440 | bytes 3743744 | tf_op jit(solution)/shard_map/hqk,khd->hqd/dot_general | solution.py:74
  113.0 0.2 copy.21
  113.1 0.5 fusion.42
  113.6 0.0 copy-start.1
  113.7 0.0 copy-start.4
  113.7 1.3 %copy-done.1 = f32[8,512,128]{2,1,0:T(8,128)} copy-done((f32[8,512,128]{2,1,0:T(8,128)}, f32[8,512,128]{2,1,0:T(8,128)S(1)}, u32[]{:S(2)}) %copy-start.1) | copy-done | bytes 2097176
  115.0 1.1 convolution_convert_fusion
  116.1 3.9 %fusion.12 = bf16[8,80,128]{2,1,0:T(8,128)(2,1)} fusion(bf16[512,8,80]{0,2,1:T(8,128)(2,1)S(1)} %bitcast.72, f32[8,512,128]{2,1,0:T(8,128)} %copy-done.1, bf16[512,8,80]{0,2,1:T(8,128)(2,1)S(1)} %bitcast.74, bf16[128,8,80]{0,2,1:T(8,128)(2,1)S(1)} %bitcast.88, f32[8,512]{1,0:T(8,128)S(1)} %get-tuple-element.13, f32[8,512]{1,0:T(8,128)S(1)} %get-tuple-element.14), kind=kOutput, calls=%fused_computation.19 | convolution fusion | flops 170557440 | bytes 3768320 | tf_op jit(solution)/shard_map/hqk,qhd->khd/dot_general | solution.py:76
  120.0 1.1 copy.22
  121.0 0.2 copy.23
  121.2 0.8 pad_maximum_fusion.1
  (11 shorter events, 0.1 us)
Async XLA Ops:
  7.4 27.1 %copy-start = (bf16[640,1280]{1,0:T(8,128)(2,1)S(1)}, bf16[640,1280]{1,0:T(8,128)(2,1)}, u32[]{:S(2)}) copy-start(bf16[640,1280]{1,0:T(8,128)(2,1)} %param.8) | copy-start | bytes 4915204
  7.4 6.3 %copy-start.5 = (s32[1,1,128]{2,1,0:T(1,128)S(1)}, s32[1,1,128]{2,1,0:T(1,128)}, u32[]{:S(2)}) copy-start(s32[1,1,128]{2,1,0:T(1,128)} %param.11) | copy-start | bytes 1540
  7.4 19.3 %reduce-scatter.2.cloned.1.call-start = ((), (), s32[]{:S(2)}) async-start(), calls=%async_computation.1 | async-start | bytes 491520 | tf_op jit(solution)/shard_map/reduce_scatter | solution.py:28
  11.5 38.2 %all-gather.5.cloned.1.call-start = ((), (), s32[]{:S(2)}) async-start(), calls=%async_computation.3 | async-start | bytes 1638400 | tf_op jit(solution)/shard_map/all_gather | solution.py:44
  13.6 90.9 %all-gather.3.cloned.1.call-start = ((), (), s32[]{:S(2)}) async-start(), calls=%async_computation.2 | async-start | bytes 3276800 | tf_op jit(solution)/shard_map/all_gather | solution.py:62
  34.4 2.4 %copy-start.3 = (bf16[1,128,3,640]{3,1,2,0:T(8,128)(2,1)S(1)}, bf16[1,128,3,640]{3,1,2,0:T(8,128)(2,1)}, u32[]{:S(2)}) copy-start(bf16[1,128,3,640]{3,1,2,0:T(8,128)(2,1)} %param.6) | copy-start | bytes 1474564
  107.3 0.8 copy-start.2
  113.6 1.3 %copy-start.1 = (f32[8,512,128]{2,1,0:T(8,128)}, f32[8,512,128]{2,1,0:T(8,128)S(1)}, u32[]{:S(2)}) copy-start(f32[8,512,128]{2,1,0:T(8,128)S(1)} %fusion.42) | copy-start | bytes 6291460
  113.7 2.4 %copy-start.4 = (bf16[1,128,1,640]{1,3,2,0:T(8,128)(2,1)S(1)}, bf16[1,128,1,640]{1,3,2,0:T(8,128)(2,1)}, u32[]{:S(2)}) copy-start(bf16[1,128,1,640]{1,3,2,0:T(8,128)(2,1)} %slice.58) | copy-start | bytes 491524
Sparse Core Ops, SparseCore 0:
  11.6 15.0 reduce-scatter.1
Sparse Core Ops, SparseCore 1:
  13.7 36.0 all-gather.4
  51.2 53.3 all-gather.2
where the time goes:
time: 130 us; the launch traced here: 129 us
  waiting for transfers between devices  63.5 us (49%)
  blocking collectives  20 us (15%)
  between operations  15 us (12%)
  local copies, waits for them, and re-layouts  12.2 us (9%)
  matrix products  12.2 us (9%)
  other arithmetic  6.42 us (5%)
    all_gather x1, waiting for transfers between devices, shards(): lax.all_gather(packed.astype(jnp.float32), 'blk', axis=0, tiled=True)  38.3 us
    all_gather x1, blocking collectives, shards(): stat_block = lax.all_gather(stats, 'blk', axis=0, tiled=True)  13.2 us
    reduce_scatter x1, waiting for transfers between devices, shards(): lax.psum_scatter((group_weight * prefix_cot[0, 0].astype(jnp.float32)).as...  13 us
    all_gather x1, waiting for transfers between devices, shards(): piece = lax.all_gather(key_value, 'blk', axis=0, tiled=True)  12.1 us
    all_gather x1, blocking collectives, shards(): total = lax.all_gather(share, 'resp', axis=0, tiled=True)  6.82 us
    dot_general x1, matrix products, shards(): jnp.einsum('hqk,qhd->khd', far_ds, far_q, preferred_element_type=jnp.floa...  3.89 us
    unnamed x14, local copies, waits for them, and re-layouts  3.62 us
    dot_general x1, matrix products, shards(): jnp.einsum('hqk,khd->hqd', near_ds, far_k, preferred_element_type=jnp.flo...  2.95 us
  transfers between devices with their start and end apart: 3, of which 3 were waited for; matrix products, arithmetic and copies ran while one was open for 7% of the time, Pallas kernels for 0%

commit v1 on v0

--- a/solution.py
+++ b/solution.py
@@ -1,12 +1,16 @@
+import functools
 import math
 
 import jax
 import jax.numpy as jnp
 from jax import lax
+from jax.experimental import pallas as pl
+from jax.experimental.pallas import tpu as pltpu
 from jax.sharding import PartitionSpec as P
 
 HD = 80
 MAXLEN = 512
+MESH = pl.DeviceIdType.MESH
 
 
 def score_pair(query, grad, log_total, delta, keys, values, scale):
@@ -17,7 +21,7 @@
     return (prob.astype(jnp.bfloat16), dscore)
 
 
-def shards(saved, prefix_cot, w_out, lengths, adv_mask, patch_map):
+def gathered(saved, prefix_cot, w_out, lengths, adv_mask, patch_map):
     rows = saved.shape[1]
     width = saved.shape[3]
     heads_here = width // HD
@@ -83,6 +87,292 @@
     return result[None]
 
 
+def kernel(
+    n_blk,
+    n_resp,
+    saved,
+    cot,
+    w_hbm,
+    lengths,
+    adv,
+    pmap,
+    out,
+    w_out,
+    qkv_t,
+    grad_t,
+    got,
+    got_cot,
+    weight,
+    got_weight,
+    prob,
+    fwd_out,
+    res,
+    back,
+    w_sem,
+    own_sem,
+    cot_sems,
+    weight_sems,
+    qkv_sems,
+    grad_sems,
+    back_sems,
+):
+    _, rows, width = saved.shape
+    hp = got.shape[1]
+    share = hp * HD
+    scale = 1.0 / math.sqrt(HD)
+    me = lax.axis_index("blk")
+    group = lax.axis_index("resp")
+    peers = [lax.rem(me + k, n_blk) for k in range(1, n_blk)]
+    partners = [lax.rem(group + k, n_resp) for k in range(1, n_resp)]
+
+    barrier = pltpu.get_barrier_semaphore()
+    for peer in peers:
+        pl.semaphore_signal(barrier, 1, device_id={"blk": peer}, device_id_type=MESH)
+    for partner in partners:
+        pl.semaphore_signal(barrier, 1, device_id={"resp": partner}, device_id_type=MESH)
+    w_copy = pltpu.make_async_copy(w_hbm, w_out, w_sem)
+    w_copy.start()
+
+    def remote(src, dst, sems, index, axis, target):
+        return pltpu.make_async_remote_copy(
+            src_ref=src,
+            dst_ref=dst,
+            send_sem=sems.at[(0, *index)],
+            recv_sem=sems.at[(1, *index)],
+            device_id={axis: target},
+            device_id_type=MESH,
+        )
+
+    def feature(owner, a):
+        return pl.ds(pl.multiple_of(owner * share + a * HD, 16), HD)
+
+    def patches(owner):
+        return pl.ds(pl.multiple_of(owner * rows, 128), rows)
+
+    for t in range(3):
+        for c in range(0, width, 128):
+            qkv_t[t, c : c + 128, :] = saved[t, :, c : c + 128].T
+
+    token = lax.broadcasted_iota(jnp.int32, (1, adv.shape[1]), 1)
+    own_weight = jnp.zeros((1, 1), jnp.float32)
+    for r in range(adv.shape[0]):
+        live = jnp.where(token < lengths[0, r], adv[r : r + 1, :], 0).astype(jnp.float32)
+        own_weight += jnp.sum(live, axis=1, keepdims=True) / MAXLEN
+    weight[...] = jnp.broadcast_to(own_weight, weight.shape)
+
+    pl.semaphore_wait(barrier, len(peers) + len(partners))
+
+    qkv_copies = [
+        [
+            remote(
+                qkv_t.at[:, feature(peer, a), :],
+                got.at[pl.ds(0, 3), a, :, patches(me)],
+                qkv_sems,
+                (a, k),
+                "blk",
+                peer,
+            )
+            for k, peer in enumerate(peers)
+        ]
+        for a in range(hp)
+    ]
+    cot_copies = [
+        remote(cot, got_cot.at[k], cot_sems, (k,), "resp", partner)
+        for k, partner in enumerate(partners)
+    ]
+    weight_copies = [
+        remote(weight, got_weight.at[k], weight_sems, (k,), "resp", partner)
+        for k, partner in enumerate(partners)
+    ]
+    own_qkv = [
+        pltpu.make_async_copy(
+            qkv_t.at[:, feature(me, a), :],
+            got.at[pl.ds(0, 3), a, :, patches(me)],
+            own_sem.at[0, a],
+        )
+        for a in range(hp)
+    ]
+    for copy in weight_copies + cot_copies + qkv_copies[0] + own_qkv:
+        copy.start()
+    for copies in qkv_copies[1:]:
+        for copy in copies:
+            copy.start()
+
+    for copy in weight_copies + cot_copies:
+        copy.wait_recv()
+    total = own_weight * cot[...].astype(jnp.float32)
+    for k in range(len(partners)):
+        total += got_weight[k, 0:1, 0:1] * got_cot[k].astype(jnp.float32)
+    w_copy.wait()
+    grad = lax.dot_general(
+        w_out[...],
+        total.astype(jnp.bfloat16),
+        (((1,), (1,)), ((), ())),
+        preferred_element_type=jnp.float32,
+    ).astype(jnp.bfloat16)
+    place = lax.broadcasted_iota(jnp.int32, (rows, rows), 0) == pmap[...]
+    grad_t[...] = jnp.dot(
+        grad, place.astype(jnp.bfloat16), preferred_element_type=jnp.float32
+    ).astype(jnp.bfloat16)
+    grad_copies = [
+        [
+            remote(
+                grad_t.at[feature(peer, a), :],
+                got.at[3, a, :, patches(me)],
+                grad_sems,
+                (a, k),
+                "blk",
+                peer,
+            )
+            for k, peer in enumerate(peers)
+        ]
+        for a in range(hp)
+    ]
+    own_grad = [
+        pltpu.make_async_copy(
+            grad_t.at[feature(me, a), :], got.at[3, a, :, patches(me)], own_sem.at[1, a]
+        )
+        for a in range(hp)
+    ]
+    for a in range(hp):
+        for copy in grad_copies[a] + [own_grad[a]]:
+            copy.start()
+
+    for a in range(hp):
+        for copy in qkv_copies[a]:
+            copy.wait_recv()
+        own_qkv[a].wait()
+        score = (
+            jnp.dot(got[1, a].T, got[0, a], preferred_element_type=jnp.float32) * scale
+        )
+        expo = jnp.exp(score - jnp.max(score, axis=0, keepdims=True))
+        inverse = 1.0 / jnp.sum(expo, axis=0, keepdims=True)
+        fwd_out[a] = (
+            jnp.dot(got[2, a], expo.astype(jnp.bfloat16), preferred_element_type=jnp.float32)
+            * inverse
+        ).astype(jnp.bfloat16)
+        prob[a] = expo * inverse
+
+    back_copies = []
+    own_back = []
+    for a in range(hp):
+        for copy in grad_copies[a]:
+            copy.wait_recv()
+        own_grad[a].wait()
+        grad = got[3, a]
+        delta = jnp.sum(
+            grad.astype(jnp.float32) * fwd_out[a].astype(jnp.float32), axis=0, keepdims=True
+        )
+        dprob = jnp.dot(got[2, a].T, grad, preferred_element_type=jnp.float32)
+        dscore = (prob[a] * (dprob - delta)).astype(jnp.bfloat16)
+        res[a, 0] = (
+            jnp.dot(got[1, a], dscore, preferred_element_type=jnp.float32) * scale
+        ).astype(jnp.bfloat16)
+        res[a, 1] = (
+            lax.dot_general(
+                got[0, a], dscore, (((1,), (1,)), ((), ())), preferred_element_type=jnp.float32
+            )
+            * scale
+        ).astype(jnp.bfloat16)
+        res[a, 2] = lax.dot_general(
+            grad,
+            prob[a].astype(jnp.bfloat16),
+            (((1,), (1,)), ((), ())),
+            preferred_element_type=jnp.float32,
+        ).astype(jnp.bfloat16)
+        for k, peer in enumerate(peers):
+            back_copies.append(
+                remote(
+                    res.at[a, :, :, patches(peer)],
+                    back.at[:, feature(me, a), :],
+                    back_sems,
+                    (a, k),
+                    "blk",
+                    peer,
+                )
+            )
+            back_copies[-1].start()
+        own_back.append(
+            pltpu.make_async_copy(
+                res.at[a, :, :, patches(me)], back.at[:, feature(me, a), :], own_sem.at[2, a]
+            )
+        )
+        own_back[-1].start()
+
+    for copy in back_copies:
+        copy.wait_recv()
+    for copy in own_back:
+        copy.wait()
+    for t in range(3):
+        for c in range(0, width, 128):
+            out[t, :, c : c + 128] = back[t, c : c + 128, :].T
+    for copy in weight_copies + cot_copies + sum(qkv_copies + grad_copies, []) + back_copies:
+        copy.wait_send()
+
+
+def exchanged(n_blk, n_resp, saved, prefix_cot, w_out, lengths, adv_mask, patch_map):
+    rows, width = saved.shape[1], saved.shape[3]
+    model = w_out.shape[1]
+    hp = width // HD // n_blk
+    count = n_blk * rows
+    bf16, f32 = jnp.bfloat16, jnp.float32
+    vmem = pl.BlockSpec(memory_space=pltpu.VMEM)
+    dma = pltpu.SemaphoreType.DMA
+    result = pl.pallas_call(
+        functools.partial(kernel, n_blk, n_resp),
+        out_shape=jax.ShapeDtypeStruct((3, rows, width), bf16),
+        in_specs=[
+            vmem,
+            vmem,
+            pl.BlockSpec(memory_space=pl.ANY),
+            pl.BlockSpec(memory_space=pltpu.SMEM),
+            vmem,
+            vmem,
+        ],
+        out_specs=vmem,
+        scratch_shapes=[
+            pltpu.VMEM((width, model), bf16),
+            pltpu.VMEM((3, width, rows), bf16),
+            pltpu.VMEM((width, rows), bf16),
+            pltpu.VMEM((4, hp, HD, count), bf16),
+            pltpu.VMEM((n_resp - 1, rows, model), bf16),
+            pltpu.VMEM((8, 128), f32),
+            pltpu.VMEM((n_resp - 1, 8, 128), f32),
+            pltpu.VMEM((hp, count, count), f32),
+            pltpu.VMEM((hp, HD, count), bf16),
+            pltpu.VMEM((hp, 3, HD, count), bf16),
+            pltpu.VMEM((3, width, rows), bf16),
+            dma,
+            dma((3, hp)),
+            dma((2, n_resp - 1)),
+            dma((2, n_resp - 1)),
+            dma((2, hp, n_blk - 1)),
+            dma((2, hp, n_blk - 1)),
+            dma((2, hp, n_blk - 1)),
+        ],
+        compiler_params=pltpu.CompilerParams(
+            collective_id=0, has_side_effects=True, vmem_limit_bytes=40 * 1024 * 1024
+        ),
+        name="prefix_backward",
+    )(
+        saved[0].transpose(1, 0, 2),
+        prefix_cot[0, 0],
+        w_out,
+        lengths,
+        adv_mask[0],
+        patch_map[0],
+    )
+    return result.transpose(1, 0, 2)[None]
+
+
+def shards(n_blk, n_resp, saved, *rest):
+    rows, width = saved.shape[1], saved.shape[3]
+    even = (width // HD) % n_blk == 0 and rows % 128 == 0 and width % 128 == 0
+    if even and n_blk > 1 and n_resp > 1:
+        return exchanged(n_blk, n_resp, saved, *rest)
+    return gathered(saved, *rest)
+
+
 def solution(mesh):
     in_specs = (
         P("dp", "blk", None, "resp"),
@@ -93,4 +383,5 @@
         P("dp", "blk", None),
     )
     out_specs = P("dp", "blk", None, "resp")
-    return jax.shard_map(shards, mesh=mesh, in_specs=in_specs, out_specs=out_specs, check_vma=False)
+    sizes = (mesh.shape["blk"], mesh.shape["resp"])
+    return jax.shard_map(functools.partial(shards, *sizes), mesh=mesh, in_specs=in_specs, out_specs=out_specs, check_vma=False)

time: 130 us -> 37.7 us (0.29)
  waiting for transfers between devices: 63.5 us -> 0 us
  Pallas kernels: 0 us -> 31.2 us
  blocking collectives: 20 us -> 0 us
  between operations: 15 us -> 0.02 us
  matrix products: 12.2 us -> 0 us
  other arithmetic: 6.42 us -> 0 us
  local copies, waits for them, and re-layouts: 12.2 us -> 6.21 us
    all_gather x2 -> x0, waiting for transfers between devices: 50.4 us -> none  [the longest x1 38.3 us: shards(): lax.all_gather(packed.astype(jnp.float32), 'blk', axis=0, tiled=True)]
    pallas_call x0 -> x1, Pallas kernels: none -> 31.2 us  [exchanged(): pl.pallas_call(functools.partial(kernel, n_blk, n_resp), out_shape=jax.Sh...]
    all_gather x2 -> x0, blocking collectives: 20 us -> none  [the longest x1 13.2 us: shards(): stat_block = lax.all_gather(stats, 'blk', axis=0, tiled=True)]
    reduce_scatter x1 -> x0, waiting for transfers between devices: 13 us -> none  [shards(): lax.psum_scatter((group_weight * prefix_cot[0, 0].astype(jnp.float32)).as...]
    dot_general x8 -> x0, matrix products: 12.2 us -> none  [the longest x1 3.89 us: shards(): jnp.einsum('hqk,qhd->khd', far_ds, far_q, preferred_element_type=jnp.floa...]
    slice x7 -> x0, local copies, waits for them, and re-layouts: 5.98 us -> none  [the longest x1 2.8 us: shards(): far_v = block[:, 2 * width:3 * width].reshape(count, heads_here, HD)]
    unnamed x14 -> x13, local copies, waits for them, and re-layouts: 3.62 us -> 6.21 us
    convert_element_type x1 -> x0, other arithmetic: 2.38 us -> none  [shards(): (group_weight * prefix_cot[0, 0].astype(jnp.float32)).astype(jnp.bfloat16)]
  transfers between devices with their start and end apart: 3 -> 0, of which waited for: 3 -> 0; matrix products, arithmetic and copies ran while one was open for 7% -> 0% of each run, Pallas kernels for 0% -> 0%
where the time goes in v1:
time: 37.7 us; the launch traced here: 37.5 us
  Pallas kernels  31.2 us (83%)
  local copies, waits for them, and re-layouts  6.21 us (16%)
    pallas_call x1, Pallas kernels, exchanged(): pl.pallas_call(functools.partial(kernel, n_blk, n_resp), out_shape=jax.Sh...  31.2 us
    unnamed x13, local copies, waits for them, and re-layouts  6.21 us

profile of v1, /device:TPU:0, one launch (start us, length us, event | category | flops | bytes accessed | tf_op | source)
XLA Modules:
  0.0 37.5 jit_solution(9754811077779459055)
XLA Ops:
  0.0 0.0 copy-start
  0.0 1.4 %copy-done = bf16[640,1280]{1,0:T(8,128)(2,1)S(1)} copy-done((bf16[640,1280]{1,0:T(8,128)(2,1)S(1)}, bf16[640,1280]{1,0:T(8,128)(2,1)}, u32[]{:S(2)}) %copy-start) | copy-done | bytes 1638424
  1.4 0.0 copy-start.1
  1.4 1.0 %copy-done.1 = bf16[1,128,3,640]{3,1,2,0:T(8,128)(2,1)S(1)} copy-done((bf16[1,128,3,640]{3,1,2,0:T(8,128)(2,1)S(1)}, bf16[1,128,3,640]{3,1,2,0:T(8,128)(2,1)}, u32[]{:S(2)}) %copy-start.1) | copy-done | bytes 491544
  2.5 0.0 copy-start.2
  2.5 1.0 %copy-done.2 = bf16[1,1,128,1280]{3,2,1,0:T(8,128)(2,1)S(1)} copy-done((bf16[1,1,128,1280]{3,2,1,0:T(8,128)(2,1)S(1)}, bf16[1,1,128,1280]{3,2,1,0:T(8,128)(2,1)}, u32[]{:S(2)}) %copy-start.2) | copy-done | bytes 327704
  3.4 0.0 copy-start.3
  3.4 0.7 %copy-done.3 = s32[1,2,512]{2,1,0:T(2,128)S(1)} copy-done((s32[1,2,512]{2,1,0:T(2,128)S(1)}, s32[1,2,512]{2,1,0:T(2,128)}, u32[]{:S(2)}) %copy-start.3) | copy-done | bytes 4120
  4.1 0.0 copy-start.4
  4.1 0.7 %copy-done.4 = s32[1,2]{1,0:T(1,128)S(1)} copy-done((s32[1,2]{1,0:T(1,128)S(1)}, s32[1,2]{1,0:T(1,128)}, u32[]{:S(2)}) %copy-start.4) | copy-done | bytes 32
  4.8 0.0 copy-start.5
  4.8 0.7 %copy-done.5 = s32[1,1,128]{2,1,0:T(1,128)S(1)} copy-done((s32[1,1,128]{2,1,0:T(1,128)S(1)}, s32[1,1,128]{2,1,0:T(1,128)}, u32[]{:S(2)}) %copy-start.5) | copy-done | bytes 536
  5.4 31.2 %prefix_backward.1 = bf16[3,128,640]{2,1,0:T(8,128)(2,1)S(1)} custom-call(bf16[3,128,640]{2,1,0:T(8,128)(2,1)S(1)} %bitcast.10, bf16[128,1280]{1,0:T(8,128)(2,1)S(1)} %bitcast.11, bf16[640,1280]{1,0:T(8,128)(2,1)S(1)} %copy-done, s32[1,2]{1,0:T(1,128)S(1)} %copy-done.4, s32[2,512]{1,0:T(2,128)S(1)} %bitcast.12, s32[1,128]{1,0:T(1,128)S(1)} %bitcast.13), custom_call_target="tpu_custom_call" | custom-call | tf_op jit(solution)/shard_map/prefix_backward/pallas_call | solution.py:321
  36.7 0.8 %copy.8 = bf16[1,128,3,640]{3,1,2,0:T(8,128)(2,1)} copy(bf16[1,128,3,640]{3,1,2,0:T(8,128)(2,1)S(1)} %bitcast.9) | data formatting | bytes 983040
Async XLA Ops:
  0.0 1.4 %copy-start = (bf16[640,1280]{1,0:T(8,128)(2,1)S(1)}, bf16[640,1280]{1,0:T(8,128)(2,1)}, u32[]{:S(2)}) copy-start(bf16[640,1280]{1,0:T(8,128)(2,1)} %w_hbm.1) | copy-start | bytes 4915204
  1.4 1.0 %copy-start.1 = (bf16[1,128,3,640]{3,1,2,0:T(8,128)(2,1)S(1)}, bf16[1,128,3,640]{3,1,2,0:T(8,128)(2,1)}, u32[]{:S(2)}) copy-start(bf16[1,128,3,640]{3,1,2,0:T(8,128)(2,1)} %param.6) | copy-start | bytes 1474564
  2.5 1.0 %copy-start.2 = (bf16[1,1,128,1280]{3,2,1,0:T(8,128)(2,1)S(1)}, bf16[1,1,128,1280]{3,2,1,0:T(8,128)(2,1)}, u32[]{:S(2)}) copy-start(bf16[1,1,128,1280]{3,2,1,0:T(8,128)(2,1)} %param.7) | copy-start | bytes 983044
  3.4 0.7 %copy-start.3 = (s32[1,2,512]{2,1,0:T(2,128)S(1)}, s32[1,2,512]{2,1,0:T(2,128)}, u32[]{:S(2)}) copy-start(s32[1,2,512]{2,1,0:T(2,128)} %param.10) | copy-start | bytes 12292
  4.1 0.7 %copy-start.4 = (s32[1,2]{1,0:T(1,128)S(1)}, s32[1,2]{1,0:T(1,128)}, u32[]{:S(2)}) copy-start(s32[1,2]{1,0:T(1,128)} %lengths.1) | copy-start | bytes 28
  4.8 0.7 %copy-start.5 = (s32[1,1,128]{2,1,0:T(1,128)S(1)}, s32[1,1,128]{2,1,0:T(1,128)}, u32[]{:S(2)}) copy-start(s32[1,1,128]{2,1,0:T(1,128)} %param.11) | copy-start | bytes 1540

commit v2 on v1

--- a/solution.py
+++ b/solution.py
@@ -90,14 +90,19 @@
 def kernel(
     n_blk,
     n_resp,
+    saved_hbm,
+    cot_hbm,
+    w_hbm,
+    lengths_hbm,
+    adv_hbm,
+    pmap_hbm,
+    out,
     saved,
     cot,
-    w_hbm,
+    w_out,
     lengths,
     adv,
     pmap,
-    out,
-    w_out,
     qkv_t,
     grad_t,
     got,
@@ -108,7 +113,7 @@
     fwd_out,
     res,
     back,
-    w_sem,
+    load_sems,
     own_sem,
     cot_sems,
     weight_sems,
@@ -130,8 +135,14 @@
         pl.semaphore_signal(barrier, 1, device_id={"blk": peer}, device_id_type=MESH)
     for partner in partners:
         pl.semaphore_signal(barrier, 1, device_id={"resp": partner}, device_id_type=MESH)
-    w_copy = pltpu.make_async_copy(w_hbm, w_out, w_sem)
-    w_copy.start()
+    pairs = [(saved_hbm.at[t], saved.at[t]) for t in range(3)]
+    pairs += [(lengths_hbm, lengths), (adv_hbm, adv), (pmap_hbm, pmap)]
+    pairs += [(cot_hbm, cot), (w_hbm, w_out)]
+    loads = [
+        pltpu.make_async_copy(src, dst, load_sems.at[n]) for n, (src, dst) in enumerate(pairs)
+    ]
+    for load in loads:
+        load.start()
 
     def remote(src, dst, sems, index, axis, target):
         return pltpu.make_async_remote_copy(
@@ -150,13 +161,16 @@
         return pl.ds(pl.multiple_of(owner * rows, 128), rows)
 
     for t in range(3):
+        loads[t].wait()
         for c in range(0, width, 128):
             qkv_t[t, c : c + 128, :] = saved[t, :, c : c + 128].T
 
+    for load in loads[3:6]:
+        load.wait()
     token = lax.broadcasted_iota(jnp.int32, (1, adv.shape[1]), 1)
     own_weight = jnp.zeros((1, 1), jnp.float32)
     for r in range(adv.shape[0]):
-        live = jnp.where(token < lengths[0, r], adv[r : r + 1, :], 0).astype(jnp.float32)
+        live = jnp.where(token < lengths[0:1, r : r + 1], adv[r : r + 1, :], 0).astype(jnp.float32)
         own_weight += jnp.sum(live, axis=1, keepdims=True) / MAXLEN
     weight[...] = jnp.broadcast_to(own_weight, weight.shape)
 
@@ -177,7 +191,7 @@
         for a in range(hp)
     ]
     cot_copies = [
-        remote(cot, got_cot.at[k], cot_sems, (k,), "resp", partner)
+        remote(cot_hbm, got_cot.at[k], cot_sems, (k,), "resp", partner)
         for k, partner in enumerate(partners)
     ]
     weight_copies = [
@@ -200,10 +214,11 @@
 
     for copy in weight_copies + cot_copies:
         copy.wait_recv()
+    for load in loads[6:]:
+        load.wait()
     total = own_weight * cot[...].astype(jnp.float32)
     for k in range(len(partners)):
         total += got_weight[k, 0:1, 0:1] * got_cot[k].astype(jnp.float32)
-    w_copy.wait()
     grad = lax.dot_general(
         w_out[...],
         total.astype(jnp.bfloat16),
@@ -316,22 +331,19 @@
     hp = width // HD // n_blk
     count = n_blk * rows
     bf16, f32 = jnp.bfloat16, jnp.float32
-    vmem = pl.BlockSpec(memory_space=pltpu.VMEM)
     dma = pltpu.SemaphoreType.DMA
     result = pl.pallas_call(
         functools.partial(kernel, n_blk, n_resp),
         out_shape=jax.ShapeDtypeStruct((3, rows, width), bf16),
-        in_specs=[
-            vmem,
-            vmem,
-            pl.BlockSpec(memory_space=pl.ANY),
-            pl.BlockSpec(memory_space=pltpu.SMEM),
-            vmem,
-            vmem,
-        ],
-        out_specs=vmem,
+        in_specs=[pl.BlockSpec(memory_space=pltpu.HBM)] * 6,
+        out_specs=pl.BlockSpec(memory_space=pltpu.VMEM),
         scratch_shapes=[
+            pltpu.VMEM((3, rows, width), bf16),
+            pltpu.VMEM((rows, model), bf16),
             pltpu.VMEM((width, model), bf16),
+            pltpu.VMEM(lengths.shape, jnp.int32),
+            pltpu.VMEM(adv_mask.shape[1:], jnp.int32),
+            pltpu.VMEM(patch_map.shape[1:], jnp.int32),
             pltpu.VMEM((3, width, rows), bf16),
             pltpu.VMEM((width, rows), bf16),
             pltpu.VMEM((4, hp, HD, count), bf16),
@@ -342,7 +354,7 @@
             pltpu.VMEM((hp, HD, count), bf16),
             pltpu.VMEM((hp, 3, HD, count), bf16),
             pltpu.VMEM((3, width, rows), bf16),
-            dma,
+            dma((8,)),
             dma((3, hp)),
             dma((2, n_resp - 1)),
             dma((2, n_resp - 1)),
@@ -355,12 +367,17 @@
         ),
         name="prefix_backward",
     )(
-        saved[0].transpose(1, 0, 2),
-        prefix_cot[0, 0],
-        w_out,
-        lengths,
-        adv_mask[0],
-        patch_map[0],
+        *(
+            pltpu.with_memory_space_constraint(array, pltpu.HBM)
+            for array in (
+                saved[0].transpose(1, 0, 2),
+                prefix_cot[0, 0],
+                w_out,
+                lengths,
+                adv_mask[0],
+                patch_map[0],
+            )
+        )
     )
     return result.transpose(1, 0, 2)[None]
 

time: 37.7 us -> 31.7 us (0.84)
  local copies, waits for them, and re-layouts: 6.21 us -> 0.78 us
  Pallas kernels: 31.2 us -> 30.8 us
    unnamed x13 -> x1, local copies, waits for them, and re-layouts: 6.21 us -> 0.78 us
    pallas_call x1, Pallas kernels: 31.2 us -> 30.8 us  [exchanged(): pl.pallas_call(functools.partial(kernel, n_blk, n_resp), out_shape=jax.Sh...]
where the time goes in v2:
time: 31.7 us; the launch traced here: 31.6 us
  Pallas kernels  30.8 us (97%)
  local copies, waits for them, and re-layouts  0.78 us (2%)
    pallas_call x1, Pallas kernels, exchanged(): pl.pallas_call(functools.partial(kernel, n_blk, n_resp), out_shape=jax.Sh...  30.8 us
    unnamed x1, local copies, waits for them, and re-layouts  0.78 us

profile of v2, /device:TPU:0, one launch (start us, length us, event | category | flops | bytes accessed | tf_op | source)
XLA Modules:
  0.0 31.6 jit_solution(9687321410725428947)
XLA Ops:
  0.0 30.8 %prefix_backward.1 = bf16[3,128,640]{2,1,0:T(8,128)(2,1)S(1)} custom-call(bf16[3,128,640]{2,1,0:T(8,128)(2,1)} %bitcast.10, bf16[128,1280]{1,0:T(8,128)(2,1)} %bitcast.11, bf16[640,1280]{1,0:T(8,128)(2,1)} %w_hbm.1, s32[1,2]{1,0:T(1,128)} %lengths_hbm.1, s32[2,512]{1,0:T(2,128)} %bitcast.12, s32[1,128]{1,0:T(1,128)} %bitcast.13), custom_call_target="tpu_custom_call" | custom-call | tf_op jit(solution)/shard_map/prefix_backward/pallas_call | solution.py:335
  30.8 0.8 %copy.8 = bf16[1,128,3,640]{3,1,2,0:T(8,128)(2,1)} copy(bf16[1,128,3,640]{3,1,2,0:T(8,128)(2,1)S(1)} %bitcast.9) | data formatting | bytes 983040

commit v3 on v2

--- a/solution.py
+++ b/solution.py
@@ -270,11 +270,39 @@
 
     back_copies = []
     own_back = []
+
+    def give_back(a, first, size):
+        for k, peer in enumerate(peers):
+            back_copies.append(
+                remote(
+                    res.at[a, pl.ds(first, size), :, patches(peer)],
+                    back.at[pl.ds(first, size), feature(me, a), :],
+                    back_sems,
+                    (first // 2, a, k),
+                    "blk",
+                    peer,
+                )
+            )
+            back_copies[-1].start()
+        own_back.append(
+            pltpu.make_async_copy(
+                res.at[a, pl.ds(first, size), :, patches(me)], back.at[pl.ds(first, size), feature(me, a), :], own_sem.at[2 + first // 2, a]
+            )
+        )
+        own_back[-1].start()
+
     for a in range(hp):
         for copy in grad_copies[a]:
             copy.wait_recv()
         own_grad[a].wait()
         grad = got[3, a]
+        res[a, 2] = lax.dot_general(
+            grad,
+            prob[a].astype(jnp.bfloat16),
+            (((1,), (1,)), ((), ())),
+            preferred_element_type=jnp.float32,
+        ).astype(jnp.bfloat16)
+        give_back(a, 2, 1)
         delta = jnp.sum(
             grad.astype(jnp.float32) * fwd_out[a].astype(jnp.float32), axis=0, keepdims=True
         )
@@ -289,30 +317,7 @@
             )
             * scale
         ).astype(jnp.bfloat16)
-        res[a, 2] = lax.dot_general(
-            grad,
-            prob[a].astype(jnp.bfloat16),
-            (((1,), (1,)), ((), ())),
-            preferred_element_type=jnp.float32,
-        ).astype(jnp.bfloat16)
-        for k, peer in enumerate(peers):
-            back_copies.append(
-                remote(
-                    res.at[a, :, :, patches(peer)],
-                    back.at[:, feature(me, a), :],
-                    back_sems,
-                    (a, k),
-                    "blk",
-                    peer,
-                )
-            )
-            back_copies[-1].start()
-        own_back.append(
-            pltpu.make_async_copy(
-                res.at[a, :, :, patches(me)], back.at[:, feature(me, a), :], own_sem.at[2, a]
-            )
-        )
-        own_back[-1].start()
+        give_back(a, 0, 2)
 
     for copy in back_copies:
         copy.wait_recv()
@@ -355,12 +360,12 @@
             pltpu.VMEM((hp, 3, HD, count), bf16),
             pltpu.VMEM((3, width, rows), bf16),
             dma((8,)),
-            dma((3, hp)),
+            dma((4, hp)),
             dma((2, n_resp - 1)),
             dma((2, n_resp - 1)),
             dma((2, hp, n_blk - 1)),
             dma((2, hp, n_blk - 1)),
-            dma((2, hp, n_blk - 1)),
+            dma((2, 2, hp, n_blk - 1)),
         ],
         compiler_params=pltpu.CompilerParams(
             collective_id=0, has_side_effects=True, vmem_limit_bytes=40 * 1024 * 1024

time: 31.7 us -> 32 us (level)
  no operation moved by 1% of the time
where the time goes in v3:
time: 32 us; the launch traced here: 31.9 us
  Pallas kernels  31.1 us (97%)
  local copies, waits for them, and re-layouts  0.78 us (2%)
    pallas_call x1, Pallas kernels, exchanged(): pl.pallas_call(functools.partial(kernel, n_blk, n_resp), out_shape=jax.Sh...  31.1 us
    unnamed x1, local copies, waits for them, and re-layouts  0.78 us

profile of v3, /device:TPU:0, one launch (start us, length us, event | category | flops | bytes accessed | tf_op | source)
XLA Modules:
  0.0 31.9 jit_solution(17194637446229790476)
XLA Ops:
  0.0 31.1 %prefix_backward.1 = bf16[3,128,640]{2,1,0:T(8,128)(2,1)S(1)} custom-call(bf16[3,128,640]{2,1,0:T(8,128)(2,1)} %bitcast.10, bf16[128,1280]{1,0:T(8,128)(2,1)} %bitcast.11, bf16[640,1280]{1,0:T(8,128)(2,1)} %w_hbm.1, s32[1,2]{1,0:T(1,128)} %lengths_hbm.1, s32[2,512]{1,0:T(2,128)} %bitcast.12, s32[1,128]{1,0:T(1,128)} %bitcast.13), custom_call_target="tpu_custom_call" | custom-call | tf_op jit(solution)/shard_map/prefix_backward/pallas_call | solution.py:340
  31.1 0.8 %copy.8 = bf16[1,128,3,640]{3,1,2,0:T(8,128)(2,1)} copy(bf16[1,128,3,640]{3,1,2,0:T(8,128)(2,1)S(1)} %bitcast.9) | data formatting | bytes 983040
